TPU v7x, 128 devices: a whole 4x4x4 slice. The times are simulated.
128 devices in a mesh: seq: 8 (over y, z_hi), head: 16 (over x, z_lo, core).
Axes of the slice: x: 4, y: 4, z: 4 (z_hi: 2, z_lo: 2; z = z_hi * 2 + z_lo), core: 2. Of those that a mesh axis runs over, the one named last changes fastest.
Arguments:
- sequence_activity: bfloat16 [2, 4096, 4096], P(None, 'seq', 'head'), may hold values from -6 to 6
- lookup_mapping_tensor: bfloat16 [4096, 16, 768], P(None, 'head'), may hold values from -1 to 1, as said below
- stepsize_mapping_matrix: bfloat16 [4096, 16], P(None, 'head'), may hold values from -0.09375 to 0.09375
- logit_sharpness: float32 [16], P('head'), may hold values from 4 to 120
- adapter_gain_vector: float32 [16, 256], P('head'), may hold values from 0.1 to 1.9
- starting_inner_left_matrix: float32 [16, 256, 512], P('head'), may hold values from -0.375 to 0.375
- starting_inner_right_matrix: float32 [16, 512, 256], P('head'), may hold values from -0.25 to 0.25
- final_mixing_matrix: bfloat16 [16, 256, 4096], P('head'), may hold values from -0.09375 to 0.09375
Outputs:
- mixed: bfloat16 [2, 4096, 4096], P(None, 'seq', 'head')
Inputs may be any that keep to these rules, and one draw needn't show every extreme that they name: `lookup_mapping_tensor`: entries of order 1 / sqrt(4096).
All inputs are finite; a program needn't handle non-finite values.
Results may differ from a plain program's by a relative error of at most 0.02.
Values may be sent and summed in bfloat16 or wider, within the bound.
A program may use at most 64 MiB of HBM per device.

v0:
```python
import jax
import jax.numpy as jnp
from jax import lax
from jax.sharding import PartitionSpec as P

WIN = 2048
NS_STEPS = 3
update_rate = 0.3


def shifted(block, axis, distance):
    devices = range(lax.axis_size(axis))
    route = [(i - distance, i) for i in devices if i - distance in devices]
    return lax.ppermute(block, axis, route)


def orthogonalize(update):
    scale = lax.rsqrt(jnp.sum(update * update) + 1e-06)
    current = update * scale
    for sweep in range(NS_STEPS):
        if current.shape[0] <= current.shape[1]:
            gram = jnp.dot(current, current.T, precision=lax.Precision.HIGHEST)
            current = 1.5 * current - 0.5 * jnp.dot(gram, current, precision=lax.Precision.HIGHEST)
        else:
            gram = jnp.dot(current.T, current, precision=lax.Precision.HIGHEST)
            current = 1.5 * current - 0.5 * jnp.dot(current, gram, precision=lax.Precision.HIGHEST)
    return current


def fast_group(weight_in, weight_out, keys, weighted, query_rows):
    in_half = weight_in.astype(jnp.bfloat16)
    out_half = weight_out.astype(jnp.bfloat16)
    hidden = jnp.dot(keys, in_half, preferred_element_type=jnp.float32)
    gating = jax.nn.sigmoid(hidden)
    activated = (hidden * gating).astype(jnp.bfloat16)
    grad_out = jnp.dot(activated.T, weighted, preferred_element_type=jnp.float32)
    backward = jnp.dot(weighted, out_half.T, preferred_element_type=jnp.float32)
    slopes = (backward * gating * (1.0 + hidden * (1.0 - gating))).astype(jnp.bfloat16)
    grad_in = jnp.dot(keys.T, slopes, preferred_element_type=jnp.float32)
    new_in = weight_in + update_rate * orthogonalize(grad_in)
    new_out = weight_out + update_rate * orthogonalize(grad_out)
    query_hidden = jnp.dot(
        query_rows, new_in.astype(jnp.bfloat16), preferred_element_type=jnp.float32
    )
    query_act = jax.nn.silu(query_hidden).astype(jnp.bfloat16)
    fast = jnp.dot(query_act, new_out.astype(jnp.bfloat16), preferred_element_type=jnp.float32)
    return (new_in, new_out, fast)


def prepare(projected, rate_col, count_seqs):
    head_dim = projected.shape[1] // 3
    query_rows = projected[:, :head_dim]
    keys = projected[:, head_dim : 2 * head_dim]
    values = projected[:, 2 * head_dim :]
    query_norm = (
        query_rows * lax.rsqrt(jnp.sum(query_rows * query_rows, axis=1, keepdims=True) + 1e-06)
    ).astype(jnp.bfloat16)
    key_norm = (keys * lax.rsqrt(jnp.sum(keys * keys, axis=1, keepdims=True) + 1e-06)).astype(
        jnp.bfloat16
    )
    value_half = values.astype(jnp.bfloat16)
    weighted = (jax.nn.softplus(rate_col) * values).astype(jnp.bfloat16)
    return (
        query_norm.reshape(count_seqs, -1, head_dim),
        key_norm.reshape(count_seqs, -1, head_dim),
        value_half.reshape(count_seqs, -1, head_dim),
        weighted.reshape(count_seqs, -1, head_dim),
    )


def attend_window(query_rows, keys, values, scale, start):
    count = query_rows.shape[1]
    window = keys.shape[1] - count
    scores = scale * jnp.einsum(
        "sqd,skd->sqk", query_rows, keys, preferred_element_type=jnp.float32
    )
    row_pos = lax.broadcasted_iota(jnp.int32, (count, count + window), 0)
    col_pos = lax.broadcasted_iota(jnp.int32, (count, count + window), 1)
    valid = (col_pos >= row_pos) & (col_pos <= row_pos + window) & (col_pos + start >= window)
    scores = jnp.where(valid[None], scores, -1e30)
    highest = jnp.max(scores, axis=2, keepdims=True)
    weights = jnp.exp(scores - highest)
    probs = (weights / jnp.sum(weights, axis=2, keepdims=True)).astype(jnp.bfloat16)
    return jnp.einsum("sqk,skd->sqd", probs, values, preferred_element_type=jnp.float32)


def combine(attended_output, fast, gain):
    normed = fast * lax.rsqrt(jnp.mean(fast * fast, axis=-1, keepdims=True) + 1e-05) * gain
    return (attended_output + normed).astype(jnp.bfloat16)


def body(
    sequence_activity,
    lookup_mapping_tensor,
    stepsize_mapping_matrix,
    logit_sharpness,
    adapter_gain_vector,
    starting_inner_left_matrix,
    starting_inner_right_matrix,
    final_mixing_matrix,
):
    seqs, head_group, local_width = sequence_activity.shape
    total_rows = seqs * head_group
    flattened = sequence_activity.reshape(total_rows, local_width)
    weights_in = lookup_mapping_tensor.reshape(
        lookup_mapping_tensor.shape[0], lookup_mapping_tensor.shape[2]
    )
    head_dim = weights_in.shape[1] // 3
    piece = lax.all_gather(flattened, "head", axis=1, tiled=True)
    projected = jnp.dot(piece, weights_in, preferred_element_type=jnp.float32)
    rate_col = jnp.dot(piece, stepsize_mapping_matrix, preferred_element_type=jnp.float32)
    query_rows, keys, values, weighted = prepare(projected, rate_col, seqs)
    token_position = lax.axis_index("seq")
    length = lax.axis_size("seq")
    reach = WIN // head_group
    hops = min(reach, length - 1)
    earlier = []
    current = (keys, values)
    for distance in range(hops):
        current = shifted((current[0], current[1]), "seq", 1)
        earlier.insert(0, current)
    windowed_key_rows = jnp.concatenate([pair[0] for pair in earlier] + [keys], axis=1)
    windowed_value_rows = jnp.concatenate([pair[1] for pair in earlier] + [values], axis=1)
    attended_output = attend_window(
        query_rows,
        windowed_key_rows,
        windowed_value_rows,
        logit_sharpness[0],
        token_position * head_group,
    )
    start_in = starting_inner_left_matrix[0]
    start_out = starting_inner_right_matrix[0]

    def turn(step, carry):
        held_in, held_out, fast_all = carry
        which = step // length
        live = step % length == token_position
        which = jnp.clip(which, 0, seqs - 1)
        use_in = jnp.where(token_position == 0, start_in, held_in)
        use_out = jnp.where(token_position == 0, start_out, held_out)
        block_keys = lax.dynamic_index_in_dim(keys, which, 0, keepdims=False)
        block_weighted = lax.dynamic_index_in_dim(weighted, which, 0, keepdims=False)
        block_queries = lax.dynamic_index_in_dim(query_rows, which, 0, keepdims=False)

        def working():
            return fast_group(use_in, use_out, block_keys, block_weighted, block_queries)

        def resting():
            return (use_in, use_out, jnp.zeros((head_group, head_dim), jnp.float32))

        new_in, new_out, fast = lax.cond(live, working, resting)
        stored = lax.dynamic_update_index_in_dim(fast_all, fast, which, 0)
        fast_all = jnp.where(live, stored, fast_all)
        sent_in, sent_out = shifted((new_in, new_out), "seq", 1)
        return (sent_in, sent_out, fast_all)

    turns = seqs * length
    carried = (start_in, start_out, jnp.zeros((seqs, head_group, head_dim), jnp.float32))
    carried = lax.fori_loop(0, turns, turn, carried)
    head_out = combine(attended_output, carried[2], adapter_gain_vector[0]).reshape(
        total_rows, head_dim
    )
    partial_value = jnp.dot(head_out, final_mixing_matrix[0], preferred_element_type=jnp.float32)
    result = lax.psum_scatter(
        partial_value.astype(jnp.bfloat16), "head", scatter_dimension=1, tiled=True
    )
    return result.reshape(seqs, head_group, -1)


def solution(mesh):
    in_specs = (
        P(None, "seq", "head"),
        P(None, "head", None),
        P(None, "head"),
        P("head"),
        P("head", None),
        P("head", None, None),
        P("head", None, None),
        P("head", None, None),
    )
    out_specs = P(None, "seq", "head")
    return jax.shard_map(body, mesh=mesh, in_specs=in_specs, out_specs=out_specs, check_vma=False)
```

profile of v0, /device:TPU:5, one launch (start us, length us, event | category | flops | bytes accessed | tf_op | source)
XLA Modules:
  0.0 1019.2 jit_solution(2209123766878446001)
XLA Ops:
  7.3 64.4 %all-gather.2.cloned.1.call-done = bf16[1024,4096]{1,0:T(8,128)(2,1)} async-done(((bf16[1024,256]{1,0:T(8,128)(2,1)}), bf16[1024,4096]{1,0:T(8,128)(2,1)}) %all-gather.2.cloned.1.call-update) | async-done | bytes 8388624 | tf_op jit(solution)/shard_map/all_gather | solution.py:109
  154.4 659.3 %while.19 = (s32[]{:T(128)}, f32[256,512]{1,0:T(8,128)}, f32[512,256]{1,0:T(8,128)}, f32[2,512,256]{2,1,0:T(8,128)}, s32[]{:T(128)}, /*index=5*/pred[]{:T(512)},...) while((s32[]{:T(128)}, f32[256,512]{1,0:T(8,128)}, ...), condition=%wide.region_9.10_spmd, body=%wide.region_4.9_spmd.sunk | while | flops 5647237120 | bytes 32771644 | solution.py:159
  156.6 24.5 %conditional.2 = (f32[256,512]{1,0:T(8,128)S(1)}, f32[512,256]{1,0:T(8,128)S(1)}, f32[1,512,256]{2,1,0:T(8,128)}) conditional(s32[]{:T(128)} %convert_element_type.110, (f32[256,512]{1,0:T(8,128)S(1)}, f32[512,256]{1,0:T(8,128)S(1)}) %tuple.60, (bf16[2,512,256]{2,1,0:T(8,128)(2,1)}, s32[]{:T(128)}, bf16[2,512,256]{2,1,0:T(8,128)(2,1)}, ...), branch_computations={%region_5.5_spmd, %region_6.8_spmd} | conditional | flops 5646843904 | bytes 23857780 | solution.py:151
  192.0 11.2 %collective-permute-done.1 = f32[512,256]{1,0:T(8,128)} collective-permute-done((f32[512,256]{1,0:T(8,128)S(1)}, f32[512,256]{1,0:T(8,128)}, u32[]{:S(2)}, u32[]{:S(2)}) %collective-permute-start.1) | collective-permute-done | bytes 524320 | tf_op jit(solution)/shard_map/while/body/eval_jaxpr/ppermute | solution.py:14
  206.4 30.1 %collective-permute-start = (f32[256,512]{1,0:T(8,128)S(1)}, f32[256,512]{1,0:T(8,128)}, u32[]{:S(2)}, u32[]{:S(2)}) collective-permute-start(f32[256,512]{1,0:T(8,128)S(1)} %get-tuple-element.431), channel_id=1, source_target_pairs={{0,16},{16,32},{32,48},{48,64},{64,80},{80,96},{96,112},{1,17},{17... | collective-permute-start | bytes 1572872 | tf_op jit(solution)/shard_map/while/body/eval_jaxpr/ppermute | solution.py:14
  244.3 11.2 %collective-permute-done.1 = f32[512,256]{1,0:T(8,128)} collective-permute-done((f32[512,256]{1,0:T(8,128)S(1)}, f32[512,256]{1,0:T(8,128)}, u32[]{:S(2)}, u32[]{:S(2)}) %collective-permute-start.1) | collective-permute-done | bytes 524320 | tf_op jit(solution)/shard_map/while/body/eval_jaxpr/ppermute | solution.py:14
  265.2 26.7 %collective-permute-start.1 = (f32[512,256]{1,0:T(8,128)S(1)}, f32[512,256]{1,0:T(8,128)}, u32[]{:S(2)}, u32[]{:S(2)}) collective-permute-start(f32[512,256]{1,0:T(8,128)S(1)} %get-tuple-element.432), channel_id=1, source_target_pairs={{0,16},{16,32},{32,48},{48,64},{64,80},{80,96},{96,112},{1,17},{17... | collective-permute-start | bytes 1572872 | tf_op jit(solution)/shard_map/while/body/eval_jaxpr/ppermute | solution.py:14
  301.9 12.3 %collective-permute-start = (f32[256,512]{1,0:T(8,128)S(1)}, f32[256,512]{1,0:T(8,128)}, u32[]{:S(2)}, u32[]{:S(2)}) collective-permute-start(f32[256,512]{1,0:T(8,128)S(1)} %get-tuple-element.431), channel_id=1, source_target_pairs={{0,16},{16,32},{32,48},{48,64},{64,80},{80,96},{96,112},{1,17},{17... | collective-permute-start | bytes 1572872 | tf_op jit(solution)/shard_map/while/body/eval_jaxpr/ppermute | solution.py:14
  335.0 20.9 %collective-permute-start = (f32[256,512]{1,0:T(8,128)S(1)}, f32[256,512]{1,0:T(8,128)}, u32[]{:S(2)}, u32[]{:S(2)}) collective-permute-start(f32[256,512]{1,0:T(8,128)S(1)} %get-tuple-element.431), channel_id=1, source_target_pairs={{0,16},{16,32},{32,48},{48,64},{64,80},{80,96},{96,112},{1,17},{17... | collective-permute-start | bytes 1572872 | tf_op jit(solution)/shard_map/while/body/eval_jaxpr/ppermute | solution.py:14
  355.9 11.5 %collective-permute-start.1 = (f32[512,256]{1,0:T(8,128)S(1)}, f32[512,256]{1,0:T(8,128)}, u32[]{:S(2)}, u32[]{:S(2)}) collective-permute-start(f32[512,256]{1,0:T(8,128)S(1)} %get-tuple-element.432), channel_id=1, source_target_pairs={{0,16},{16,32},{32,48},{48,64},{64,80},{80,96},{96,112},{1,17},{17... | collective-permute-start | bytes 1572872 | tf_op jit(solution)/shard_map/while/body/eval_jaxpr/ppermute | solution.py:14
  375.9 12.2 %collective-permute-start = (f32[256,512]{1,0:T(8,128)S(1)}, f32[256,512]{1,0:T(8,128)}, u32[]{:S(2)}, u32[]{:S(2)}) collective-permute-start(f32[256,512]{1,0:T(8,128)S(1)} %get-tuple-element.431), channel_id=1, source_target_pairs={{0,16},{16,32},{32,48},{48,64},{64,80},{80,96},{96,112},{1,17},{17... | collective-permute-start | bytes 1572872 | tf_op jit(solution)/shard_map/while/body/eval_jaxpr/ppermute | solution.py:14
  388.1 21.2 %collective-permute-start.1 = (f32[512,256]{1,0:T(8,128)S(1)}, f32[512,256]{1,0:T(8,128)}, u32[]{:S(2)}, u32[]{:S(2)}) collective-permute-start(f32[512,256]{1,0:T(8,128)S(1)} %get-tuple-element.432), channel_id=1, source_target_pairs={{0,16},{16,32},{32,48},{48,64},{64,80},{80,96},{96,112},{1,17},{17... | collective-permute-start | bytes 1572872 | tf_op jit(solution)/shard_map/while/body/eval_jaxpr/ppermute | solution.py:14
  417.9 12.6 %collective-permute-start = (f32[256,512]{1,0:T(8,128)S(1)}, f32[256,512]{1,0:T(8,128)}, u32[]{:S(2)}, u32[]{:S(2)}) collective-permute-start(f32[256,512]{1,0:T(8,128)S(1)} %get-tuple-element.431), channel_id=1, source_target_pairs={{0,16},{16,32},{32,48},{48,64},{64,80},{80,96},{96,112},{1,17},{17... | collective-permute-start | bytes 1572872 | tf_op jit(solution)/shard_map/while/body/eval_jaxpr/ppermute | solution.py:14
  430.5 11.8 %collective-permute-start.1 = (f32[512,256]{1,0:T(8,128)S(1)}, f32[512,256]{1,0:T(8,128)}, u32[]{:S(2)}, u32[]{:S(2)}) collective-permute-start(f32[512,256]{1,0:T(8,128)S(1)} %get-tuple-element.432), channel_id=1, source_target_pairs={{0,16},{16,32},{32,48},{48,64},{64,80},{80,96},{96,112},{1,17},{17... | collective-permute-start | bytes 1572872 | tf_op jit(solution)/shard_map/while/body/eval_jaxpr/ppermute | solution.py:14
  451.4 19.6 %collective-permute-start = (f32[256,512]{1,0:T(8,128)S(1)}, f32[256,512]{1,0:T(8,128)}, u32[]{:S(2)}, u32[]{:S(2)}) collective-permute-start(f32[256,512]{1,0:T(8,128)S(1)} %get-tuple-element.431), channel_id=1, source_target_pairs={{0,16},{16,32},{32,48},{48,64},{64,80},{80,96},{96,112},{1,17},{17... | collective-permute-start | bytes 1572872 | tf_op jit(solution)/shard_map/while/body/eval_jaxpr/ppermute | solution.py:14
  471.0 12.4 %collective-permute-start.1 = (f32[512,256]{1,0:T(8,128)S(1)}, f32[512,256]{1,0:T(8,128)}, u32[]{:S(2)}, u32[]{:S(2)}) collective-permute-start(f32[512,256]{1,0:T(8,128)S(1)} %get-tuple-element.432), channel_id=1, source_target_pairs={{0,16},{16,32},{32,48},{48,64},{64,80},{80,96},{96,112},{1,17},{17... | collective-permute-start | bytes 1572872 | tf_op jit(solution)/shard_map/while/body/eval_jaxpr/ppermute | solution.py:14
  492.1 24.5 %conditional.2 = (f32[256,512]{1,0:T(8,128)S(1)}, f32[512,256]{1,0:T(8,128)S(1)}, f32[1,512,256]{2,1,0:T(8,128)}) conditional(s32[]{:T(128)} %convert_element_type.110, (f32[256,512]{1,0:T(8,128)S(1)}, f32[512,256]{1,0:T(8,128)S(1)}) %tuple.60, (bf16[2,512,256]{2,1,0:T(8,128)(2,1)}, s32[]{:T(128)}, bf16[2,512,256]{2,1,0:T(8,128)(2,1)}, ...), branch_computations={%region_5.5_spmd, %region_6.8_spmd} | conditional | flops 5646843904 | bytes 23857780 | solution.py:151
  537.8 33.1 %collective-permute-start = (f32[256,512]{1,0:T(8,128)S(1)}, f32[256,512]{1,0:T(8,128)}, u32[]{:S(2)}, u32[]{:S(2)}) collective-permute-start(f32[256,512]{1,0:T(8,128)S(1)} %get-tuple-element.431), channel_id=1, source_target_pairs={{0,16},{16,32},{32,48},{48,64},{64,80},{80,96},{96,112},{1,17},{17... | collective-permute-start | bytes 1572872 | tf_op jit(solution)/shard_map/while/body/eval_jaxpr/ppermute | solution.py:14
  596.2 26.8 %collective-permute-start.1 = (f32[512,256]{1,0:T(8,128)S(1)}, f32[512,256]{1,0:T(8,128)}, u32[]{:S(2)}, u32[]{:S(2)}) collective-permute-start(f32[512,256]{1,0:T(8,128)S(1)} %get-tuple-element.432), channel_id=1, source_target_pairs={{0,16},{16,32},{32,48},{48,64},{64,80},{80,96},{96,112},{1,17},{17... | collective-permute-start | bytes 1572872 | tf_op jit(solution)/shard_map/while/body/eval_jaxpr/ppermute | solution.py:14
  661.3 21.5 %collective-permute-start = (f32[256,512]{1,0:T(8,128)S(1)}, f32[256,512]{1,0:T(8,128)}, u32[]{:S(2)}, u32[]{:S(2)}) collective-permute-start(f32[256,512]{1,0:T(8,128)S(1)} %get-tuple-element.431), channel_id=1, source_target_pairs={{0,16},{16,32},{32,48},{48,64},{64,80},{80,96},{96,112},{1,17},{17... | collective-permute-start | bytes 1572872 | tf_op jit(solution)/shard_map/while/body/eval_jaxpr/ppermute | solution.py:14
  712.5 21.1 %collective-permute-start.1 = (f32[512,256]{1,0:T(8,128)S(1)}, f32[512,256]{1,0:T(8,128)}, u32[]{:S(2)}, u32[]{:S(2)}) collective-permute-start(f32[512,256]{1,0:T(8,128)S(1)} %get-tuple-element.432), channel_id=1, source_target_pairs={{0,16},{16,32},{32,48},{48,64},{64,80},{80,96},{96,112},{1,17},{17... | collective-permute-start | bytes 1572872 | tf_op jit(solution)/shard_map/while/body/eval_jaxpr/ppermute | solution.py:14
  742.1 13.7 %collective-permute-start = (f32[256,512]{1,0:T(8,128)S(1)}, f32[256,512]{1,0:T(8,128)}, u32[]{:S(2)}, u32[]{:S(2)}) collective-permute-start(f32[256,512]{1,0:T(8,128)S(1)} %get-tuple-element.431), channel_id=1, source_target_pairs={{0,16},{16,32},{32,48},{48,64},{64,80},{80,96},{96,112},{1,17},{17... | collective-permute-start | bytes 1572872 | tf_op jit(solution)/shard_map/while/body/eval_jaxpr/ppermute | solution.py:14
  775.7 16.5 %collective-permute-start = (f32[256,512]{1,0:T(8,128)S(1)}, f32[256,512]{1,0:T(8,128)}, u32[]{:S(2)}, u32[]{:S(2)}) collective-permute-start(f32[256,512]{1,0:T(8,128)S(1)} %get-tuple-element.431), channel_id=1, source_target_pairs={{0,16},{16,32},{32,48},{48,64},{64,80},{80,96},{96,112},{1,17},{17... | collective-permute-start | bytes 1572872 | tf_op jit(solution)/shard_map/while/body/eval_jaxpr/ppermute | solution.py:14
  853.3 159.1 %reduce-scatter.2.cloned.1.call-done = bf16[1024,256]{1,0:T(8,128)(2,1)} async-done(((bf16[1024,4096]{1,0:T(8,128)(2,1)}), bf16[1024,256]{1,0:T(8,128)(2,1)}) %reduce-scatter.2.cloned.1.call-update) | async-done | bytes 524304 | tf_op jit(solution)/shard_map/reduce_scatter | solution.py:164
  (229 shorter events, 444.2 us)
Async XLA Ops:
  6.5 65.2 %all-gather.2.cloned.1.call-start = ((), (), s32[]{:S(2)}) async-start(), calls=%async_computation.1 | async-start | bytes 8912896 | tf_op jit(solution)/shard_map/all_gather | solution.py:109
  7.3 1005.1 %reduce-scatter.2.cloned.1.call-start = ((), (), s32[]{:S(2)}) async-start(), calls=%async_computation.2 | async-start | bytes 8912896 | tf_op jit(solution)/shard_map/reduce_scatter | solution.py:164
  101.9 22.5 %collective-permute-start.7 = (bf16[2,512,256]{2,1,0:T(8,128)(2,1)S(1)}, bf16[2,512,256]{2,1,0:T(8,128)(2,1)}, u32[]{:S(2)}, u32[]{:S(2)}) collective-permute-start(bf16[2,512,256]{2,1,0:T(8,128)(2,1)S(1)} %collective-permute-done.6), channel_id=1, source_target_pairs={{0,16},{16,32},{32,48},{48,64},{64,80},{80,96},{96,112},{1,17},{17... | collective-permute-start | bytes 1572872 | tf_op jit(solution)/shard_map/ppermute | solution.py:14
  113.2 22.4 %collective-permute-start.3 = (bf16[2,512,256]{2,1,0:T(8,128)(2,1)S(1)}, bf16[2,512,256]{2,1,0:T(8,128)(2,1)}, u32[]{:S(2)}, u32[]{:S(2)}) collective-permute-start(bf16[2,512,256]{2,1,0:T(8,128)(2,1)S(1)} %collective-permute-done.2), channel_id=1, source_target_pairs={{0,16},{16,32},{32,48},{48,64},{64,80},{80,96},{96,112},{1,17},{17... | collective-permute-start | bytes 1572872 | tf_op jit(solution)/shard_map/ppermute | solution.py:14
  124.3 22.6 %collective-permute-start.8 = (bf16[2,512,256]{2,1,0:T(8,128)(2,1)}, bf16[2,512,256]{2,1,0:T(8,128)(2,1)}, u32[]{:S(2)}, u32[]{:S(2)}) collective-permute-start(bf16[2,512,256]{2,1,0:T(8,128)(2,1)} %collective-permute-done.7), channel_id=1, source_target_pairs={{0,16},{16,32},{32,48},{48,64},{64,80},{80,96},{96,112},{1,17},{17... | collective-permute-start | bytes 1572872 | tf_op jit(solution)/shard_map/ppermute | solution.py:14
  135.6 679.7 %collective-permute-start.4 = (bf16[2,512,256]{2,1,0:T(8,128)(2,1)}, bf16[2,512,256]{2,1,0:T(8,128)(2,1)}, u32[]{:S(2)}, u32[]{:S(2)}) collective-permute-start(bf16[2,512,256]{2,1,0:T(8,128)(2,1)} %collective-permute-done.3), channel_id=1, source_target_pairs={{0,16},{16,32},{32,48},{48,64},{64,80},{80,96},{96,112},{1,17},{17... | collective-permute-start | bytes 1572872 | tf_op jit(solution)/shard_map/ppermute | solution.py:14
  146.9 674.4 %collective-permute-start.9 = (bf16[2,512,256]{2,1,0:T(8,128)(2,1)}, bf16[2,512,256]{2,1,0:T(8,128)(2,1)}, u32[]{:S(2)}, u32[]{:S(2)}) collective-permute-start(bf16[2,512,256]{2,1,0:T(8,128)(2,1)} %collective-permute-done.8), channel_id=1, source_target_pairs={{0,16},{16,32},{32,48},{48,64},{64,80},{80,96},{96,112},{1,17},{17... | collective-permute-start | bytes 1572872 | tf_op jit(solution)/shard_map/ppermute | solution.py:14
  206.4 37.9 %collective-permute-start = (f32[256,512]{1,0:T(8,128)S(1)}, f32[256,512]{1,0:T(8,128)}, u32[]{:S(2)}, u32[]{:S(2)}) collective-permute-start(f32[256,512]{1,0:T(8,128)S(1)} %get-tuple-element.431), channel_id=1, source_target_pairs={{0,16},{16,32},{32,48},{48,64},{64,80},{80,96},{96,112},{1,17},{17... | collective-permute-start | bytes 1572872 | tf_op jit(solution)/shard_map/while/body/eval_jaxpr/ppermute | solution.py:14
  258.7 35.1 %collective-permute-start = (f32[256,512]{1,0:T(8,128)S(1)}, f32[256,512]{1,0:T(8,128)}, u32[]{:S(2)}, u32[]{:S(2)}) collective-permute-start(f32[256,512]{1,0:T(8,128)S(1)} %get-tuple-element.431), channel_id=1, source_target_pairs={{0,16},{16,32},{32,48},{48,64},{64,80},{80,96},{96,112},{1,17},{17... | collective-permute-start | bytes 1572872 | tf_op jit(solution)/shard_map/while/body/eval_jaxpr/ppermute | solution.py:14
  265.2 33.6 %collective-permute-start.1 = (f32[512,256]{1,0:T(8,128)S(1)}, f32[512,256]{1,0:T(8,128)}, u32[]{:S(2)}, u32[]{:S(2)}) collective-permute-start(f32[512,256]{1,0:T(8,128)S(1)} %get-tuple-element.432), channel_id=1, source_target_pairs={{0,16},{16,32},{32,48},{48,64},{64,80},{80,96},{96,112},{1,17},{17... | collective-permute-start | bytes 1572872 | tf_op jit(solution)/shard_map/while/body/eval_jaxpr/ppermute | solution.py:14
  335.0 34.3 %collective-permute-start = (f32[256,512]{1,0:T(8,128)S(1)}, f32[256,512]{1,0:T(8,128)}, u32[]{:S(2)}, u32[]{:S(2)}) collective-permute-start(f32[256,512]{1,0:T(8,128)S(1)} %get-tuple-element.431), channel_id=1, source_target_pairs={{0,16},{16,32},{32,48},{48,64},{64,80},{80,96},{96,112},{1,17},{17... | collective-permute-start | bytes 1572872 | tf_op jit(solution)/shard_map/while/body/eval_jaxpr/ppermute | solution.py:14
  375.9 35.4 %collective-permute-start = (f32[256,512]{1,0:T(8,128)S(1)}, f32[256,512]{1,0:T(8,128)}, u32[]{:S(2)}, u32[]{:S(2)}) collective-permute-start(f32[256,512]{1,0:T(8,128)S(1)} %get-tuple-element.431), channel_id=1, source_target_pairs={{0,16},{16,32},{32,48},{48,64},{64,80},{80,96},{96,112},{1,17},{17... | collective-permute-start | bytes 1572872 | tf_op jit(solution)/shard_map/while/body/eval_jaxpr/ppermute | solution.py:14
  388.1 26.5 %collective-permute-start.1 = (f32[512,256]{1,0:T(8,128)S(1)}, f32[512,256]{1,0:T(8,128)}, u32[]{:S(2)}, u32[]{:S(2)}) collective-permute-start(f32[512,256]{1,0:T(8,128)S(1)} %get-tuple-element.432), channel_id=1, source_target_pairs={{0,16},{16,32},{32,48},{48,64},{64,80},{80,96},{96,112},{1,17},{17... | collective-permute-start | bytes 1572872 | tf_op jit(solution)/shard_map/while/body/eval_jaxpr/ppermute | solution.py:14
  417.9 26.4 %collective-permute-start = (f32[256,512]{1,0:T(8,128)S(1)}, f32[256,512]{1,0:T(8,128)}, u32[]{:S(2)}, u32[]{:S(2)}) collective-permute-start(f32[256,512]{1,0:T(8,128)S(1)} %get-tuple-element.431), channel_id=1, source_target_pairs={{0,16},{16,32},{32,48},{48,64},{64,80},{80,96},{96,112},{1,17},{17... | collective-permute-start | bytes 1572872 | tf_op jit(solution)/shard_map/while/body/eval_jaxpr/ppermute | solution.py:14
  451.4 34.0 %collective-permute-start = (f32[256,512]{1,0:T(8,128)S(1)}, f32[256,512]{1,0:T(8,128)}, u32[]{:S(2)}, u32[]{:S(2)}) collective-permute-start(f32[256,512]{1,0:T(8,128)S(1)} %get-tuple-element.431), channel_id=1, source_target_pairs={{0,16},{16,32},{32,48},{48,64},{64,80},{80,96},{96,112},{1,17},{17... | collective-permute-start | bytes 1572872 | tf_op jit(solution)/shard_map/while/body/eval_jaxpr/ppermute | solution.py:14
  537.8 38.4 %collective-permute-start = (f32[256,512]{1,0:T(8,128)S(1)}, f32[256,512]{1,0:T(8,128)}, u32[]{:S(2)}, u32[]{:S(2)}) collective-permute-start(f32[256,512]{1,0:T(8,128)S(1)} %get-tuple-element.431), channel_id=1, source_target_pairs={{0,16},{16,32},{32,48},{48,64},{64,80},{80,96},{96,112},{1,17},{17... | collective-permute-start | bytes 1572872 | tf_op jit(solution)/shard_map/while/body/eval_jaxpr/ppermute | solution.py:14
  589.7 35.2 %collective-permute-start = (f32[256,512]{1,0:T(8,128)S(1)}, f32[256,512]{1,0:T(8,128)}, u32[]{:S(2)}, u32[]{:S(2)}) collective-permute-start(f32[256,512]{1,0:T(8,128)S(1)} %get-tuple-element.431), channel_id=1, source_target_pairs={{0,16},{16,32},{32,48},{48,64},{64,80},{80,96},{96,112},{1,17},{17... | collective-permute-start | bytes 1572872 | tf_op jit(solution)/shard_map/while/body/eval_jaxpr/ppermute | solution.py:14
  596.2 32.1 %collective-permute-start.1 = (f32[512,256]{1,0:T(8,128)S(1)}, f32[512,256]{1,0:T(8,128)}, u32[]{:S(2)}, u32[]{:S(2)}) collective-permute-start(f32[512,256]{1,0:T(8,128)S(1)} %get-tuple-element.432), channel_id=1, source_target_pairs={{0,16},{16,32},{32,48},{48,64},{64,80},{80,96},{96,112},{1,17},{17... | collective-permute-start | bytes 1572872 | tf_op jit(solution)/shard_map/while/body/eval_jaxpr/ppermute | solution.py:14
  661.3 32.5 %collective-permute-start = (f32[256,512]{1,0:T(8,128)S(1)}, f32[256,512]{1,0:T(8,128)}, u32[]{:S(2)}, u32[]{:S(2)}) collective-permute-start(f32[256,512]{1,0:T(8,128)S(1)} %get-tuple-element.431), channel_id=1, source_target_pairs={{0,16},{16,32},{32,48},{48,64},{64,80},{80,96},{96,112},{1,17},{17... | collective-permute-start | bytes 1572872 | tf_op jit(solution)/shard_map/while/body/eval_jaxpr/ppermute | solution.py:14
  706.0 29.5 %collective-permute-start = (f32[256,512]{1,0:T(8,128)S(1)}, f32[256,512]{1,0:T(8,128)}, u32[]{:S(2)}, u32[]{:S(2)}) collective-permute-start(f32[256,512]{1,0:T(8,128)S(1)} %get-tuple-element.431), channel_id=1, source_target_pairs={{0,16},{16,32},{32,48},{48,64},{64,80},{80,96},{96,112},{1,17},{17... | collective-permute-start | bytes 1572872 | tf_op jit(solution)/shard_map/while/body/eval_jaxpr/ppermute | solution.py:14
  712.5 26.4 %collective-permute-start.1 = (f32[512,256]{1,0:T(8,128)S(1)}, f32[512,256]{1,0:T(8,128)}, u32[]{:S(2)}, u32[]{:S(2)}) collective-permute-start(f32[512,256]{1,0:T(8,128)S(1)} %get-tuple-element.432), channel_id=1, source_target_pairs={{0,16},{16,32},{32,48},{48,64},{64,80},{80,96},{96,112},{1,17},{17... | collective-permute-start | bytes 1572872 | tf_op jit(solution)/shard_map/while/body/eval_jaxpr/ppermute | solution.py:14
  742.1 22.3 %collective-permute-start = (f32[256,512]{1,0:T(8,128)S(1)}, f32[256,512]{1,0:T(8,128)}, u32[]{:S(2)}, u32[]{:S(2)}) collective-permute-start(f32[256,512]{1,0:T(8,128)S(1)} %get-tuple-element.431), channel_id=1, source_target_pairs={{0,16},{16,32},{32,48},{48,64},{64,80},{80,96},{96,112},{1,17},{17... | collective-permute-start | bytes 1572872 | tf_op jit(solution)/shard_map/while/body/eval_jaxpr/ppermute | solution.py:14
  775.7 29.3 %collective-permute-start = (f32[256,512]{1,0:T(8,128)S(1)}, f32[256,512]{1,0:T(8,128)}, u32[]{:S(2)}, u32[]{:S(2)}) collective-permute-start(f32[256,512]{1,0:T(8,128)S(1)} %get-tuple-element.431), channel_id=1, source_target_pairs={{0,16},{16,32},{32,48},{48,64},{64,80},{80,96},{96,112},{1,17},{17... | collective-permute-start | bytes 1572872 | tf_op jit(solution)/shard_map/while/body/eval_jaxpr/ppermute | solution.py:14
  792.1 21.6 %collective-permute-start.1 = (f32[512,256]{1,0:T(8,128)S(1)}, f32[512,256]{1,0:T(8,128)}, u32[]{:S(2)}, u32[]{:S(2)}) collective-permute-start(f32[512,256]{1,0:T(8,128)S(1)} %get-tuple-element.432), channel_id=1, source_target_pairs={{0,16},{16,32},{32,48},{48,64},{64,80},{80,96},{96,112},{1,17},{17... | collective-permute-start | bytes 1572872 | tf_op jit(solution)/shard_map/while/body/eval_jaxpr/ppermute | solution.py:14
  (32 other events, 1300.0 us)
Sparse Core Ops, SparseCore 0:
  9.0 62.6 all-gather.1
  853.4 158.8 reduce-scatter.1
where the time goes:
time: 1020 us
  starting transfers between devices  455 us (45%)
  waiting for transfers between devices  366 us (36%)
  matrix products  81.7 us (8%)
  other arithmetic  72.6 us (7%)
  local copies, waits for them, and re-layouts  25.6 us (3%)
  between operations  14.3 us (1%)
    ppermute x40, starting transfers between devices, shifted(): return lax.ppermute(block, axis, route)  455 us
    reduce_scatter x1, waiting for transfers between devices, body(): lax.psum_scatter(partial_value.astype(jnp.bfloat16), 'head', scatter_dime...  159 us
    ppermute x40, waiting for transfers between devices, shifted(): return lax.ppermute(block, axis, route)  142 us
    all_gather x1, waiting for transfers between devices, body(): piece = lax.all_gather(flattened, 'head', axis=1, tiled=True)  64.4 us
    select_n x16, other arithmetic, turn(): fast_all = jnp.where(live, stored, fast_all)  30.8 us
  transfers between devices with their start and end apart: 42, of which 27 were waited for; matrix products, arithmetic and copies ran while one was open for 14% of the time, Pallas kernels for 0%

commit v1 on v0

--- a/solution.py
+++ b/solution.py
@@ -106,7 +106,8 @@
         lookup_mapping_tensor.shape[0], lookup_mapping_tensor.shape[2]
     )
     head_dim = weights_in.shape[1] // 3
-    piece = lax.all_gather(flattened, "head", axis=1, tiled=True)
+    repeated = jnp.stack([flattened] * lax.axis_size("head"))
+    piece = jnp.concatenate(lax.all_to_all(repeated, "head", 0, 0), axis=1)
     projected = jnp.dot(piece, weights_in, preferred_element_type=jnp.float32)
     rate_col = jnp.dot(piece, stepsize_mapping_matrix, preferred_element_type=jnp.float32)
     query_rows, keys, values, weighted = prepare(projected, rate_col, seqs)

time: 1020 us -> 1060 us (1.039)
  blocking collectives: 0 us -> 99 us
  waiting for transfers between devices: 366 us -> 311 us
  local copies, waits for them, and re-layouts: 25.6 us -> 39.8 us
  starting transfers between devices: 455 us -> 441 us
    all_to_all x0 -> x1, blocking collectives: none -> 99 us  [body(): piece = jnp.concatenate(lax.all_to_all(repeated, 'head', 0, 0), axis=1)]
    all_gather x1 -> x0, waiting for transfers between devices: 64.4 us -> none  [body(): piece = lax.all_gather(flattened, 'head', axis=1, tiled=True)]
    ppermute x40, starting transfers between devices: 455 us -> 441 us  [shifted(): return lax.ppermute(block, axis, route)]
    cond x4 -> x22, local copies, waits for them, and re-layouts: 0.01 us -> 11.3 us
  transfers between devices with their start and end apart: 42 -> 41, of which waited for: 27 -> 27; matrix products, arithmetic and copies ran while one was open for 14% -> 14% of each run, Pallas kernels for 0% -> 0%
where the time goes in v1:
time: 1060 us
  starting transfers between devices  441 us (42%)
  waiting for transfers between devices  311 us (29%)
  blocking collectives  99 us (9%)
  matrix products  77.3 us (7%)
  other arithmetic  72.6 us (7%)
  local copies, waits for them, and re-layouts  39.8 us (4%)
  between operations  14.3 us (1%)
    ppermute x40, starting transfers between devices, shifted(): return lax.ppermute(block, axis, route)  441 us
    reduce_scatter x1, waiting for transfers between devices, body(): lax.psum_scatter(partial_value.astype(jnp.bfloat16), 'head', scatter_dime...  166 us
    ppermute x40, waiting for transfers between devices, shifted(): return lax.ppermute(block, axis, route)  145 us
    all_to_all x1, blocking collectives, body(): piece = jnp.concatenate(lax.all_to_all(repeated, 'head', 0, 0), axis=1)  99 us
    select_n x16, other arithmetic, turn(): fast_all = jnp.where(live, stored, fast_all)  30.9 us
  transfers between devices with their start and end apart: 41, of which 27 were waited for; matrix products, arithmetic and copies ran while one was open for 14% of the time, Pallas kernels for 0%

profile of v1, /device:TPU:5, one launch (start us, length us, event | category | flops | bytes accessed | tf_op | source)
XLA Modules:
  0.0 1058.9 jit_solution(14762903156389281950)
XLA Ops:
  9.0 99.0 %all_to_all.5 = bf16[16,1024,256]{1,2,0:T(8,128)(2,1)S(1)} all-to-all(bf16[16,1024,256]{1,2,0:T(8,128)(2,1)S(1)} %stack.3), channel_id=1, replica_groups=mesh['seq'=8,'head'=16] {'head'}, dimensions={0} | all-to-all | bytes 16777216 | tf_op jit(solution)/shard_map/all_to_all | solution.py:110
  187.6 660.8 %while.19 = (s32[]{:T(128)}, f32[256,512]{1,0:T(8,128)S(1)}, f32[512,256]{1,0:T(8,128)}, f32[2,512,256]{2,1,0:T(8,128)}, s32[]{:T(128)}, /*index=5*/pred[]{:T(51...) while((s32[]{:T(128)}, f32[256,512]{1,0:T(8,128)S(1)}, ...), condition=%wide.region_9.10_spmd, body=%wide.region_4.9_spmd.sunk | while | flops 5647237120 | bytes 36965468 | solution.py:160
  189.8 26.2 %conditional.2 = (f32[256,512]{1,0:T(8,128)S(1)}, f32[512,256]{1,0:T(8,128)}, f32[1,512,256]{2,1,0:T(8,128)}) conditional(s32[]{:T(128)} %convert_element_type.110, (f32[256,512]{1,0:T(8,128)S(1)}, f32[512,256]{1,0:T(8,128)S(1)}) %tuple.60, (bf16[2,512,256]{2,1,0:T(8,128)(2,1)}, s32[]{:T(128)}, bf16[2,512,256]{2,1,0:T(8,128)(2,1)}, ...), branch_computations={%region_5.5_spmd, %region_6.8_spmd} | conditional | flops 5646843904 | bytes 28051604 | solution.py:152
  226.2 11.3 %collective-permute-done.1 = f32[512,256]{1,0:T(8,128)} collective-permute-done((f32[512,256]{1,0:T(8,128)}, f32[512,256]{1,0:T(8,128)}, u32[]{:S(2)}, u32[]{:S(2)}) %collective-permute-start.1) | collective-permute-done | bytes 524320 | tf_op jit(solution)/shard_map/while/body/eval_jaxpr/ppermute | solution.py:14
  241.4 29.1 %collective-permute-start = (f32[256,512]{1,0:T(8,128)S(1)}, f32[256,512]{1,0:T(8,128)S(1)}, u32[]{:S(2)}, u32[]{:S(2)}) collective-permute-start(f32[256,512]{1,0:T(8,128)S(1)} %get-tuple-element.431), channel_id=1, source_target_pairs={{0,16},{16,32},{32,48},{48,64},{64,80},{80,96},{96,112},{1,17},{17... | collective-permute-start | bytes 1572872 | tf_op jit(solution)/shard_map/while/body/eval_jaxpr/ppermute | solution.py:14
  278.6 11.3 %collective-permute-done.1 = f32[512,256]{1,0:T(8,128)} collective-permute-done((f32[512,256]{1,0:T(8,128)}, f32[512,256]{1,0:T(8,128)}, u32[]{:S(2)}, u32[]{:S(2)}) %collective-permute-start.1) | collective-permute-done | bytes 524320 | tf_op jit(solution)/shard_map/while/body/eval_jaxpr/ppermute | solution.py:14
  298.4 28.4 %collective-permute-start.1 = (f32[512,256]{1,0:T(8,128)}, f32[512,256]{1,0:T(8,128)}, u32[]{:S(2)}, u32[]{:S(2)}) collective-permute-start(f32[512,256]{1,0:T(8,128)} %get-tuple-element.432), channel_id=1, source_target_pairs={{0,16},{16,32},{32,48},{48,64},{64,80},{80,96},{96,112},{1,17},{17... | collective-permute-start | bytes 1572872 | tf_op jit(solution)/shard_map/while/body/eval_jaxpr/ppermute | solution.py:14
  370.0 19.5 %collective-permute-start = (f32[256,512]{1,0:T(8,128)S(1)}, f32[256,512]{1,0:T(8,128)S(1)}, u32[]{:S(2)}, u32[]{:S(2)}) collective-permute-start(f32[256,512]{1,0:T(8,128)S(1)} %get-tuple-element.431), channel_id=1, source_target_pairs={{0,16},{16,32},{32,48},{48,64},{64,80},{80,96},{96,112},{1,17},{17... | collective-permute-start | bytes 1572872 | tf_op jit(solution)/shard_map/while/body/eval_jaxpr/ppermute | solution.py:14
  389.5 12.1 %collective-permute-start.1 = (f32[512,256]{1,0:T(8,128)}, f32[512,256]{1,0:T(8,128)}, u32[]{:S(2)}, u32[]{:S(2)}) collective-permute-start(f32[512,256]{1,0:T(8,128)} %get-tuple-element.432), channel_id=1, source_target_pairs={{0,16},{16,32},{32,48},{48,64},{64,80},{80,96},{96,112},{1,17},{17... | collective-permute-start | bytes 1572872 | tf_op jit(solution)/shard_map/while/body/eval_jaxpr/ppermute | solution.py:14
  421.3 22.8 %collective-permute-start.1 = (f32[512,256]{1,0:T(8,128)}, f32[512,256]{1,0:T(8,128)}, u32[]{:S(2)}, u32[]{:S(2)}) collective-permute-start(f32[512,256]{1,0:T(8,128)} %get-tuple-element.432), channel_id=1, source_target_pairs={{0,16},{16,32},{32,48},{48,64},{64,80},{80,96},{96,112},{1,17},{17... | collective-permute-start | bytes 1572872 | tf_op jit(solution)/shard_map/while/body/eval_jaxpr/ppermute | solution.py:14
  453.6 11.1 %collective-permute-start = (f32[256,512]{1,0:T(8,128)S(1)}, f32[256,512]{1,0:T(8,128)S(1)}, u32[]{:S(2)}, u32[]{:S(2)}) collective-permute-start(f32[256,512]{1,0:T(8,128)S(1)} %get-tuple-element.431), channel_id=1, source_target_pairs={{0,16},{16,32},{32,48},{48,64},{64,80},{80,96},{96,112},{1,17},{17... | collective-permute-start | bytes 1572872 | tf_op jit(solution)/shard_map/while/body/eval_jaxpr/ppermute | solution.py:14
  464.7 11.7 %collective-permute-start.1 = (f32[512,256]{1,0:T(8,128)}, f32[512,256]{1,0:T(8,128)}, u32[]{:S(2)}, u32[]{:S(2)}) collective-permute-start(f32[512,256]{1,0:T(8,128)} %get-tuple-element.432), channel_id=1, source_target_pairs={{0,16},{16,32},{32,48},{48,64},{64,80},{80,96},{96,112},{1,17},{17... | collective-permute-start | bytes 1572872 | tf_op jit(solution)/shard_map/while/body/eval_jaxpr/ppermute | solution.py:14
  486.9 18.3 %collective-permute-start = (f32[256,512]{1,0:T(8,128)S(1)}, f32[256,512]{1,0:T(8,128)S(1)}, u32[]{:S(2)}, u32[]{:S(2)}) collective-permute-start(f32[256,512]{1,0:T(8,128)S(1)} %get-tuple-element.431), channel_id=1, source_target_pairs={{0,16},{16,32},{32,48},{48,64},{64,80},{80,96},{96,112},{1,17},{17... | collective-permute-start | bytes 1572872 | tf_op jit(solution)/shard_map/while/body/eval_jaxpr/ppermute | solution.py:14
  505.3 14.1 %collective-permute-start.1 = (f32[512,256]{1,0:T(8,128)}, f32[512,256]{1,0:T(8,128)}, u32[]{:S(2)}, u32[]{:S(2)}) collective-permute-start(f32[512,256]{1,0:T(8,128)} %get-tuple-element.432), channel_id=1, source_target_pairs={{0,16},{16,32},{32,48},{48,64},{64,80},{80,96},{96,112},{1,17},{17... | collective-permute-start | bytes 1572872 | tf_op jit(solution)/shard_map/while/body/eval_jaxpr/ppermute | solution.py:14
  527.8 26.2 %conditional.2 = (f32[256,512]{1,0:T(8,128)S(1)}, f32[512,256]{1,0:T(8,128)}, f32[1,512,256]{2,1,0:T(8,128)}) conditional(s32[]{:T(128)} %convert_element_type.110, (f32[256,512]{1,0:T(8,128)S(1)}, f32[512,256]{1,0:T(8,128)S(1)}) %tuple.60, (bf16[2,512,256]{2,1,0:T(8,128)(2,1)}, s32[]{:T(128)}, bf16[2,512,256]{2,1,0:T(8,128)(2,1)}, ...), branch_computations={%region_5.5_spmd, %region_6.8_spmd} | conditional | flops 5646843904 | bytes 28051604 | solution.py:152
  561.4 10.7 %collective-permute-done.1 = f32[512,256]{1,0:T(8,128)} collective-permute-done((f32[512,256]{1,0:T(8,128)}, f32[512,256]{1,0:T(8,128)}, u32[]{:S(2)}, u32[]{:S(2)}) %collective-permute-start.1) | collective-permute-done | bytes 524320 | tf_op jit(solution)/shard_map/while/body/eval_jaxpr/ppermute | solution.py:14
  575.9 30.7 %collective-permute-start = (f32[256,512]{1,0:T(8,128)S(1)}, f32[256,512]{1,0:T(8,128)S(1)}, u32[]{:S(2)}, u32[]{:S(2)}) collective-permute-start(f32[256,512]{1,0:T(8,128)S(1)} %get-tuple-element.431), channel_id=1, source_target_pairs={{0,16},{16,32},{32,48},{48,64},{64,80},{80,96},{96,112},{1,17},{17... | collective-permute-start | bytes 1572872 | tf_op jit(solution)/shard_map/while/body/eval_jaxpr/ppermute | solution.py:14
  612.7 10.4 collective-permute-done.1
  631.5 28.4 %collective-permute-start.1 = (f32[512,256]{1,0:T(8,128)}, f32[512,256]{1,0:T(8,128)}, u32[]{:S(2)}, u32[]{:S(2)}) collective-permute-start(f32[512,256]{1,0:T(8,128)} %get-tuple-element.432), channel_id=1, source_target_pairs={{0,16},{16,32},{32,48},{48,64},{64,80},{80,96},{96,112},{1,17},{17... | collective-permute-start | bytes 1572872 | tf_op jit(solution)/shard_map/while/body/eval_jaxpr/ppermute | solution.py:14
  698.5 20.8 %collective-permute-start = (f32[256,512]{1,0:T(8,128)S(1)}, f32[256,512]{1,0:T(8,128)S(1)}, u32[]{:S(2)}, u32[]{:S(2)}) collective-permute-start(f32[256,512]{1,0:T(8,128)S(1)} %get-tuple-element.431), channel_id=1, source_target_pairs={{0,16},{16,32},{32,48},{48,64},{64,80},{80,96},{96,112},{1,17},{17... | collective-permute-start | bytes 1572872 | tf_op jit(solution)/shard_map/while/body/eval_jaxpr/ppermute | solution.py:14
  748.1 23.1 %collective-permute-start.1 = (f32[512,256]{1,0:T(8,128)}, f32[512,256]{1,0:T(8,128)}, u32[]{:S(2)}, u32[]{:S(2)}) collective-permute-start(f32[512,256]{1,0:T(8,128)} %get-tuple-element.432), channel_id=1, source_target_pairs={{0,16},{16,32},{32,48},{48,64},{64,80},{80,96},{96,112},{1,17},{17... | collective-permute-start | bytes 1572872 | tf_op jit(solution)/shard_map/while/body/eval_jaxpr/ppermute | solution.py:14
  780.6 10.7 %collective-permute-start = (f32[256,512]{1,0:T(8,128)S(1)}, f32[256,512]{1,0:T(8,128)S(1)}, u32[]{:S(2)}, u32[]{:S(2)}) collective-permute-start(f32[256,512]{1,0:T(8,128)S(1)} %get-tuple-element.431), channel_id=1, source_target_pairs={{0,16},{16,32},{32,48},{48,64},{64,80},{80,96},{96,112},{1,17},{17... | collective-permute-start | bytes 1572872 | tf_op jit(solution)/shard_map/while/body/eval_jaxpr/ppermute | solution.py:14
  811.9 17.1 %collective-permute-start = (f32[256,512]{1,0:T(8,128)S(1)}, f32[256,512]{1,0:T(8,128)S(1)}, u32[]{:S(2)}, u32[]{:S(2)}) collective-permute-start(f32[256,512]{1,0:T(8,128)S(1)} %get-tuple-element.431), channel_id=1, source_target_pairs={{0,16},{16,32},{32,48},{48,64},{64,80},{80,96},{96,112},{1,17},{17... | collective-permute-start | bytes 1572872 | tf_op jit(solution)/shard_map/while/body/eval_jaxpr/ppermute | solution.py:14
  886.0 166.1 %reduce-scatter.2.cloned.1.call-done = bf16[1024,256]{1,0:T(8,128)(2,1)} async-done(((bf16[1024,4096]{1,0:T(8,128)(2,1)}), bf16[1024,256]{1,0:T(8,128)(2,1)}) %reduce-scatter.2.cloned.1.call-update) | async-done | bytes 524304 | tf_op jit(solution)/shard_map/reduce_scatter | solution.py:165
  (244 shorter events, 457.6 us)
Async XLA Ops:
  6.5 1045.5 %reduce-scatter.2.cloned.1.call-start = ((), (), s32[]{:S(2)}) async-start(), calls=%async_computation.2 | async-start | bytes 8912896 | tf_op jit(solution)/shard_map/reduce_scatter | solution.py:165
  124.9 21.4 %collective-permute-start.6 = (bf16[2,512,256]{2,1,0:T(8,128)(2,1)S(1)}, bf16[2,512,256]{2,1,0:T(8,128)(2,1)}, u32[]{:S(2)}, u32[]{:S(2)}) collective-permute-start(bf16[2,512,256]{2,1,0:T(8,128)(2,1)S(1)} %bitcast.75), channel_id=1, source_target_pairs={{0,16},{16,32},{32,48},{48,64},{64,80},{80,96},{96,112},{1,17},{17... | collective-permute-start | bytes 1572872 | tf_op jit(solution)/shard_map/ppermute | solution.py:14
  135.1 22.5 %collective-permute-start.3 = (bf16[2,512,256]{2,1,0:T(8,128)(2,1)}, bf16[2,512,256]{2,1,0:T(8,128)(2,1)}, u32[]{:S(2)}, u32[]{:S(2)}) collective-permute-start(bf16[2,512,256]{2,1,0:T(8,128)(2,1)} %collective-permute-done.2), channel_id=1, source_target_pairs={{0,16},{16,32},{32,48},{48,64},{64,80},{80,96},{96,112},{1,17},{17... | collective-permute-start | bytes 1572872 | tf_op jit(solution)/shard_map/ppermute | solution.py:14
  146.3 22.6 %collective-permute-start.7 = (bf16[2,512,256]{2,1,0:T(8,128)(2,1)}, bf16[2,512,256]{2,1,0:T(8,128)(2,1)}, u32[]{:S(2)}, u32[]{:S(2)}) collective-permute-start(bf16[2,512,256]{2,1,0:T(8,128)(2,1)} %collective-permute-done.6), channel_id=1, source_target_pairs={{0,16},{16,32},{32,48},{48,64},{64,80},{80,96},{96,112},{1,17},{17... | collective-permute-start | bytes 1572872 | tf_op jit(solution)/shard_map/ppermute | solution.py:14
  157.6 22.5 %collective-permute-start.4 = (bf16[2,512,256]{2,1,0:T(8,128)(2,1)}, bf16[2,512,256]{2,1,0:T(8,128)(2,1)}, u32[]{:S(2)}, u32[]{:S(2)}) collective-permute-start(bf16[2,512,256]{2,1,0:T(8,128)(2,1)} %collective-permute-done.3), channel_id=1, source_target_pairs={{0,16},{16,32},{32,48},{48,64},{64,80},{80,96},{96,112},{1,17},{17... | collective-permute-start | bytes 1572872 | tf_op jit(solution)/shard_map/ppermute | solution.py:14
  168.8 681.0 %collective-permute-start.8 = (bf16[2,512,256]{2,1,0:T(8,128)(2,1)}, bf16[2,512,256]{2,1,0:T(8,128)(2,1)}, u32[]{:S(2)}, u32[]{:S(2)}) collective-permute-start(bf16[2,512,256]{2,1,0:T(8,128)(2,1)} %collective-permute-done.7), channel_id=1, source_target_pairs={{0,16},{16,32},{32,48},{48,64},{64,80},{80,96},{96,112},{1,17},{17... | collective-permute-start | bytes 1572872 | tf_op jit(solution)/shard_map/ppermute | solution.py:14
  180.1 675.5 %collective-permute-start.5 = (bf16[2,512,256]{2,1,0:T(8,128)(2,1)}, bf16[2,512,256]{2,1,0:T(8,128)(2,1)}, u32[]{:S(2)}, u32[]{:S(2)}) collective-permute-start(bf16[2,512,256]{2,1,0:T(8,128)(2,1)} %collective-permute-done.4), channel_id=1, source_target_pairs={{0,16},{16,32},{32,48},{48,64},{64,80},{80,96},{96,112},{1,17},{17... | collective-permute-start | bytes 1572872 | tf_op jit(solution)/shard_map/ppermute | solution.py:14
  241.4 37.1 %collective-permute-start = (f32[256,512]{1,0:T(8,128)S(1)}, f32[256,512]{1,0:T(8,128)S(1)}, u32[]{:S(2)}, u32[]{:S(2)}) collective-permute-start(f32[256,512]{1,0:T(8,128)S(1)} %get-tuple-element.431), channel_id=1, source_target_pairs={{0,16},{16,32},{32,48},{48,64},{64,80},{80,96},{96,112},{1,17},{17... | collective-permute-start | bytes 1572872 | tf_op jit(solution)/shard_map/while/body/eval_jaxpr/ppermute | solution.py:14
  293.8 34.9 %collective-permute-start = (f32[256,512]{1,0:T(8,128)S(1)}, f32[256,512]{1,0:T(8,128)S(1)}, u32[]{:S(2)}, u32[]{:S(2)}) collective-permute-start(f32[256,512]{1,0:T(8,128)S(1)} %get-tuple-element.431), channel_id=1, source_target_pairs={{0,16},{16,32},{32,48},{48,64},{64,80},{80,96},{96,112},{1,17},{17... | collective-permute-start | bytes 1572872 | tf_op jit(solution)/shard_map/while/body/eval_jaxpr/ppermute | solution.py:14
  298.4 35.0 %collective-permute-start.1 = (f32[512,256]{1,0:T(8,128)}, f32[512,256]{1,0:T(8,128)}, u32[]{:S(2)}, u32[]{:S(2)}) collective-permute-start(f32[512,256]{1,0:T(8,128)} %get-tuple-element.432), channel_id=1, source_target_pairs={{0,16},{16,32},{32,48},{48,64},{64,80},{80,96},{96,112},{1,17},{17... | collective-permute-start | bytes 1572872 | tf_op jit(solution)/shard_map/while/body/eval_jaxpr/ppermute | solution.py:14
  370.0 33.5 %collective-permute-start = (f32[256,512]{1,0:T(8,128)S(1)}, f32[256,512]{1,0:T(8,128)S(1)}, u32[]{:S(2)}, u32[]{:S(2)}) collective-permute-start(f32[256,512]{1,0:T(8,128)S(1)} %get-tuple-element.431), channel_id=1, source_target_pairs={{0,16},{16,32},{32,48},{48,64},{64,80},{80,96},{96,112},{1,17},{17... | collective-permute-start | bytes 1572872 | tf_op jit(solution)/shard_map/while/body/eval_jaxpr/ppermute | solution.py:14
  411.4 34.7 %collective-permute-start = (f32[256,512]{1,0:T(8,128)S(1)}, f32[256,512]{1,0:T(8,128)S(1)}, u32[]{:S(2)}, u32[]{:S(2)}) collective-permute-start(f32[256,512]{1,0:T(8,128)S(1)} %get-tuple-element.431), channel_id=1, source_target_pairs={{0,16},{16,32},{32,48},{48,64},{64,80},{80,96},{96,112},{1,17},{17... | collective-permute-start | bytes 1572872 | tf_op jit(solution)/shard_map/while/body/eval_jaxpr/ppermute | solution.py:14
  421.3 28.5 %collective-permute-start.1 = (f32[512,256]{1,0:T(8,128)}, f32[512,256]{1,0:T(8,128)}, u32[]{:S(2)}, u32[]{:S(2)}) collective-permute-start(f32[512,256]{1,0:T(8,128)} %get-tuple-element.432), channel_id=1, source_target_pairs={{0,16},{16,32},{32,48},{48,64},{64,80},{80,96},{96,112},{1,17},{17... | collective-permute-start | bytes 1572872 | tf_op jit(solution)/shard_map/while/body/eval_jaxpr/ppermute | solution.py:14
  453.6 24.7 %collective-permute-start = (f32[256,512]{1,0:T(8,128)S(1)}, f32[256,512]{1,0:T(8,128)S(1)}, u32[]{:S(2)}, u32[]{:S(2)}) collective-permute-start(f32[256,512]{1,0:T(8,128)S(1)} %get-tuple-element.431), channel_id=1, source_target_pairs={{0,16},{16,32},{32,48},{48,64},{64,80},{80,96},{96,112},{1,17},{17... | collective-permute-start | bytes 1572872 | tf_op jit(solution)/shard_map/while/body/eval_jaxpr/ppermute | solution.py:14
  486.9 34.3 %collective-permute-start = (f32[256,512]{1,0:T(8,128)S(1)}, f32[256,512]{1,0:T(8,128)S(1)}, u32[]{:S(2)}, u32[]{:S(2)}) collective-permute-start(f32[256,512]{1,0:T(8,128)S(1)} %get-tuple-element.431), channel_id=1, source_target_pairs={{0,16},{16,32},{32,48},{48,64},{64,80},{80,96},{96,112},{1,17},{17... | collective-permute-start | bytes 1572872 | tf_op jit(solution)/shard_map/while/body/eval_jaxpr/ppermute | solution.py:14
  505.3 20.3 %collective-permute-start.1 = (f32[512,256]{1,0:T(8,128)}, f32[512,256]{1,0:T(8,128)}, u32[]{:S(2)}, u32[]{:S(2)}) collective-permute-start(f32[512,256]{1,0:T(8,128)} %get-tuple-element.432), channel_id=1, source_target_pairs={{0,16},{16,32},{32,48},{48,64},{64,80},{80,96},{96,112},{1,17},{17... | collective-permute-start | bytes 1572872 | tf_op jit(solution)/shard_map/while/body/eval_jaxpr/ppermute | solution.py:14
  575.9 36.8 %collective-permute-start = (f32[256,512]{1,0:T(8,128)S(1)}, f32[256,512]{1,0:T(8,128)S(1)}, u32[]{:S(2)}, u32[]{:S(2)}) collective-permute-start(f32[256,512]{1,0:T(8,128)S(1)} %get-tuple-element.431), channel_id=1, source_target_pairs={{0,16},{16,32},{32,48},{48,64},{64,80},{80,96},{96,112},{1,17},{17... | collective-permute-start | bytes 1572872 | tf_op jit(solution)/shard_map/while/body/eval_jaxpr/ppermute | solution.py:14
  627.0 34.8 %collective-permute-start = (f32[256,512]{1,0:T(8,128)S(1)}, f32[256,512]{1,0:T(8,128)S(1)}, u32[]{:S(2)}, u32[]{:S(2)}) collective-permute-start(f32[256,512]{1,0:T(8,128)S(1)} %get-tuple-element.431), channel_id=1, source_target_pairs={{0,16},{16,32},{32,48},{48,64},{64,80},{80,96},{96,112},{1,17},{17... | collective-permute-start | bytes 1572872 | tf_op jit(solution)/shard_map/while/body/eval_jaxpr/ppermute | solution.py:14
  631.5 34.1 %collective-permute-start.1 = (f32[512,256]{1,0:T(8,128)}, f32[512,256]{1,0:T(8,128)}, u32[]{:S(2)}, u32[]{:S(2)}) collective-permute-start(f32[512,256]{1,0:T(8,128)} %get-tuple-element.432), channel_id=1, source_target_pairs={{0,16},{16,32},{32,48},{48,64},{64,80},{80,96},{96,112},{1,17},{17... | collective-permute-start | bytes 1572872 | tf_op jit(solution)/shard_map/while/body/eval_jaxpr/ppermute | solution.py:14
  698.5 32.1 %collective-permute-start = (f32[256,512]{1,0:T(8,128)S(1)}, f32[256,512]{1,0:T(8,128)S(1)}, u32[]{:S(2)}, u32[]{:S(2)}) collective-permute-start(f32[256,512]{1,0:T(8,128)S(1)} %get-tuple-element.431), channel_id=1, source_target_pairs={{0,16},{16,32},{32,48},{48,64},{64,80},{80,96},{96,112},{1,17},{17... | collective-permute-start | bytes 1572872 | tf_op jit(solution)/shard_map/while/body/eval_jaxpr/ppermute | solution.py:14
  719.3 20.4 %collective-permute-start.1 = (f32[512,256]{1,0:T(8,128)}, f32[512,256]{1,0:T(8,128)}, u32[]{:S(2)}, u32[]{:S(2)}) collective-permute-start(f32[512,256]{1,0:T(8,128)} %get-tuple-element.432), channel_id=1, source_target_pairs={{0,16},{16,32},{32,48},{48,64},{64,80},{80,96},{96,112},{1,17},{17... | collective-permute-start | bytes 1572872 | tf_op jit(solution)/shard_map/while/body/eval_jaxpr/ppermute | solution.py:14
  743.6 29.5 %collective-permute-start = (f32[256,512]{1,0:T(8,128)S(1)}, f32[256,512]{1,0:T(8,128)S(1)}, u32[]{:S(2)}, u32[]{:S(2)}) collective-permute-start(f32[256,512]{1,0:T(8,128)S(1)} %get-tuple-element.431), channel_id=1, source_target_pairs={{0,16},{16,32},{32,48},{48,64},{64,80},{80,96},{96,112},{1,17},{17... | collective-permute-start | bytes 1572872 | tf_op jit(solution)/shard_map/while/body/eval_jaxpr/ppermute | solution.py:14
  748.1 28.7 %collective-permute-start.1 = (f32[512,256]{1,0:T(8,128)}, f32[512,256]{1,0:T(8,128)}, u32[]{:S(2)}, u32[]{:S(2)}) collective-permute-start(f32[512,256]{1,0:T(8,128)} %get-tuple-element.432), channel_id=1, source_target_pairs={{0,16},{16,32},{32,48},{48,64},{64,80},{80,96},{96,112},{1,17},{17... | collective-permute-start | bytes 1572872 | tf_op jit(solution)/shard_map/while/body/eval_jaxpr/ppermute | solution.py:14
  811.9 29.3 %collective-permute-start = (f32[256,512]{1,0:T(8,128)S(1)}, f32[256,512]{1,0:T(8,128)S(1)}, u32[]{:S(2)}, u32[]{:S(2)}) collective-permute-start(f32[256,512]{1,0:T(8,128)S(1)} %get-tuple-element.431), channel_id=1, source_target_pairs={{0,16},{16,32},{32,48},{48,64},{64,80},{80,96},{96,112},{1,17},{17... | collective-permute-start | bytes 1572872 | tf_op jit(solution)/shard_map/while/body/eval_jaxpr/ppermute | solution.py:14
  (31 other events, 1461.3 us)
Sparse Core Ops, SparseCore 0:
  886.1 165.9 reduce-scatter.1
